TPU v7x, 32 devices: a whole 2x2x4 slice. The times are simulated.
32 devices in a mesh: blk: 8 (over z, y), dir: 4 (over x, core).
Axes of the slice: x: 2, y: 2, z: 4, core: 2. Of those that a mesh axis runs over, the one named last changes fastest.
Arguments:
- spectrum: float32 [36, 36, 128, 128], P('dir', None, 'blk'), may hold values from 0 to 4.5, as said below
- group_speed: float32 [36, 128, 128], P(None, 'blk'), may hold values from 0.3 to 1
- ocean_current: float32 [2, 128, 128], P(None, 'blk'), may hold values from -0.5 to 0.5
- route_slot: int32 [128, 128], P('blk'), may hold values from -1 to 2047, as said below
- wind_vector: float32 [8, 2, 2048], P('blk'), may hold values from -4 to 4
- ice_cover: float32 [8, 2048], P('blk'), may hold values from 0 to 0.9
Outputs:
- spectrum_out: float32 [36, 36, 128, 128], P('dir', None, 'blk')
- ocean_forcing: float32 [4, 128, 128], P('dir', 'blk')
Inputs may be any that keep to these rules, and one draw needn't show every extreme that they name: `route_slot`: on one geographic block the sea cells routed to one owner use slots 0 to their count - 1, at most 256 of them; some owner receives 256 cells from every block. Land cells hold -1. `spectrum`: positive everywhere.
All inputs are finite; a program needn't handle non-finite values.
Results may differ from a plain program's by a relative error of at most 0.00002.
Values sent between devices are 32-bit elements; how exact they have to be, the bound alone decides.
A program may use at most 64 MiB of HBM per device.

v0:
```python
import jax
import jax.numpy as jnp
from jax import lax
from jax.sharding import PartitionSpec as P

COURANT = 0.15
WIND_GROWTH = 0.15
DAMP_RATE = 0.5
STEEP_COEF = 0.01
STRESS_SCALE = 1.0
STOKES_SCALE = 0.15
RATIO_STEP = 1.1


def with_halo(value, sides, width):
    for axis, dim in sides:
        size, length = (lax.axis_size(axis), value.shape[dim])
        up = [(i, (i + 1) % size) for i in range(size - 1)]
        down = [(j, i) for i, j in up]
        last = lax.slice_in_dim(value, length - width, length, axis=dim)
        initial = lax.slice_in_dim(value, 0, width, axis=dim)
        before = lax.ppermute(last, axis, up)
        after = lax.ppermute(initial, axis, down)
        value = jnp.concatenate([before, value, after], axis=dim)
    return value


def flux_difference(energy, velocity, open_mask, along):
    count = energy.shape[along] - 1
    low_energy = lax.slice_in_dim(energy, 0, count, axis=along)
    high_energy = lax.slice_in_dim(energy, 1, count + 1, axis=along)
    face_speed = 0.5 * (
        lax.slice_in_dim(velocity, 0, count, axis=along)
        + lax.slice_in_dim(velocity, 1, count + 1, axis=along)
    )
    face_open = lax.slice_in_dim(open_mask, 0, count, axis=along) * lax.slice_in_dim(
        open_mask, 1, count + 1, axis=along
    )
    flux = face_open * (
        jnp.maximum(face_speed, 0.0) * low_energy + jnp.minimum(face_speed, 0.0) * high_energy
    )
    return lax.slice_in_dim(flux, 1, count, axis=along) - lax.slice_in_dim(
        flux, 0, count - 1, axis=along
    )


def source_terms(
    flat_energy, wind_here, ice_here, cosine_dir, sine_dir, ratios, dir_here, freq_count
):
    point_count = flat_energy.shape[1]
    energy = flat_energy.reshape(dir_here, freq_count, point_count)
    ratio_square = ratios * ratios
    ratio_cube = ratio_square * ratios
    moment_band = jnp.sum(energy * ratio_square[None, :, None], axis=(0, 1))
    moment = lax.psum(moment_band, "dir")
    steepness = STEEP_COEF * moment
    damping = DAMP_RATE * steepness / (1.0 + steepness)
    wind_gain = (
        WIND_GROWTH
        * (1.0 - ice_here)[None, :]
        * jnp.maximum(
            wind_here[0][None, :] * cosine_dir[:, None] + wind_here[1][None, :] * sine_dir[:, None],
            0.0,
        )
    )
    growth = ratios[None, :, None] * (wind_gain - damping[None, :])[:, None, :]
    updated = energy * (1.0 + growth)
    stress_dir = jnp.sum(ratio_square[None, :, None] * wind_gain[:, None, :] * energy, axis=1)
    stokes_dir = jnp.sum(ratio_cube[None, :, None] * updated, axis=1)
    partial_value = jnp.stack(
        [
            STRESS_SCALE * jnp.sum(cosine_dir[:, None] * stress_dir, axis=0),
            STRESS_SCALE * jnp.sum(sine_dir[:, None] * stress_dir, axis=0),
            STOKES_SCALE * jnp.sum(cosine_dir[:, None] * stokes_dir, axis=0),
            STOKES_SCALE * jnp.sum(sine_dir[:, None] * stokes_dir, axis=0),
        ]
    )
    return (updated.reshape(dir_here * freq_count, point_count), partial_value)


def on_device(spectrum, group_speed, ocean_current, route_slot, wind_vector, ice_cover):
    blocks = lax.axis_size("blk")
    band_count = lax.axis_size("dir")
    dir_here, freq_count, rows_here, width_y = spectrum.shape
    cell_count = rows_here * width_y
    capacity = cell_count // blocks
    bin_count = dir_here * freq_count
    currents = lax.all_to_all(ocean_current, "blk", split_axis=2, concat_axis=1, tiled=True)
    currents = jnp.transpose(currents, (0, 2, 1))
    sea_mask = (route_slot >= 0).astype(jnp.float32)
    stacked = jnp.concatenate(
        [spectrum.reshape(bin_count, rows_here, width_y), group_speed, currents, sea_mask[None]],
        axis=0,
    )
    padded = with_halo(stacked, (("blk", 1),), 1)
    energy_x = padded[:bin_count].reshape(dir_here, freq_count, rows_here + 2, width_y)
    speed_x = padded[bin_count : bin_count + freq_count]
    flow_x = padded[bin_count + freq_count]
    mask_x = padded[bin_count + freq_count + 2]
    global_dir = (lax.axis_index("dir") * dir_here + jnp.arange(dir_here, dtype=jnp.int32)).astype(
        jnp.float32
    )
    angles = 2.0 * jnp.pi * global_dir / (dir_here * band_count)
    cosine_dir = jnp.cos(angles)
    sine_dir = jnp.sin(angles)
    ratios = jnp.power(
        jnp.float32(RATIO_STEP), jnp.arange(freq_count, dtype=jnp.float32) - (freq_count - 1)
    )
    velocity_x = speed_x[None] * cosine_dir[:, None, None, None] + flow_x[None, None]
    div_x = flux_difference(
        energy_x, velocity_x, jnp.broadcast_to(mask_x[None, None], energy_x.shape), 2
    )
    velocity_y = group_speed[None] * sine_dir[:, None, None, None] + currents[1][None, None]
    widths = ((0, 0), (0, 0), (0, 0), (1, 1))
    energy_y = jnp.pad(spectrum, widths)
    mask_y = jnp.broadcast_to(jnp.pad(sea_mask, ((0, 0), (1, 1)))[None, None], energy_y.shape)
    div_y = flux_difference(energy_y, jnp.pad(velocity_y, widths), mask_y, 3)
    moved = sea_mask[None, None] * (spectrum - COURANT * (div_x + div_y))
    flat = moved.reshape(bin_count, cell_count)
    slot_index = jnp.where(route_slot >= 0, route_slot, cell_count).reshape(cell_count)
    wind_back, ice_back = (
        lax.all_to_all(
            wind_vector[0].reshape(2, blocks, capacity),
            "blk",
            split_axis=1,
            concat_axis=1,
            tiled=True,
        ),
        lax.all_to_all(
            ice_cover.reshape(1, blocks, capacity), "blk", split_axis=1, concat_axis=1, tiled=True
        ),
    )
    wind_geo = jnp.take(
        wind_back.reshape(2, cell_count), slot_index, axis=1, mode="fill", fill_value=0.0
    )
    ice_geo = jnp.take(
        ice_back.reshape(1, cell_count), slot_index, axis=1, mode="fill", fill_value=0.0
    )
    result, partial_geo = source_terms(
        flat, wind_geo, ice_geo[0], cosine_dir, sine_dir, ratios, dir_here, freq_count
    )
    own_share = 4 // band_count
    summed = lax.psum(partial_geo, "dir")
    own_parts = lax.dynamic_slice_in_dim(summed, lax.axis_index("dir") * own_share, own_share, 0)
    ocean_grid = jnp.transpose(own_parts.reshape(own_share, rows_here, width_y), (0, 2, 1))
    ocean_part = lax.all_to_all(ocean_grid, "blk", split_axis=1, concat_axis=2, tiled=True)
    return (result.reshape(dir_here, freq_count, rows_here, width_y), ocean_part)


def solution(mesh):
    return jax.shard_map(
        on_device,
        mesh=mesh,
        in_specs=(
            P("dir", None, "blk", None),
            P(None, "blk", None),
            P(None, "blk", None),
            P("blk", None),
            P("blk", None, None),
            P("blk", None),
        ),
        out_specs=(P("dir", None, "blk", None), P("dir", "blk", None)),
        check_vma=False,
    )
```

profile of v0, /device:TPU:0, one launch (start us, length us, event | category | flops | bytes accessed | tf_op | source)
XLA Modules:
  0.0 107.1 jit_solution(5997870882728222305)
XLA Ops:
  0.6 7.3 %all-to-all-start.1 = ((f32[1,8,256]{2,0,1:T(1,128)}), f32[1,8,256]{2,0,1:T(1,128)S(1)}, u32[]{:S(2)}, u32[]{:S(2)}) async-start(f32[1,8,256]{2,0,1:T(1,128)} %bitcast.89), calls=%async_computation.1 | async-start | bytes 16384 | tf_op jit(solution)/shard_map/all_to_all | solution.py:129
  7.9 0.7 fusion.22
  9.3 1.3 %compare_and_fusion = pred[2048]{0:T(1024)(128)(4,1)} fusion(s32[16,128]{1,0:T(8,128)} %param.9), kind=kLoop, calls=%fused_computation.75 | loop fusion | flops 16384 | bytes 10240 | tf_op jit(solution)/shard_map/jit(_take)/and | solution.py:136
  13.1 0.8 copy.19
  13.9 0.8 reshape.355
  14.7 6.0 %all-to-all-start = ((f32[8,1,512]{2,1,0:T(1,128)}), f32[8,1,512]{2,1,0:T(1,128)S(1)}, u32[]{:S(2)}, u32[]{:S(2)}) async-start(f32[8,1,512]{2,1,0:T(1,128)} %reshape.355), calls=%async_computation | async-start | bytes 32768 | tf_op jit(solution)/shard_map/all_to_all | solution.py:88
  20.8 11.8 %gather_fusion = f32[2048]{0:T(1024)S(1)} fusion(f32[2048]{0:T(1024)S(1)} %bitcast.57, s32[2048]{0:T(1024)S(1)} %broadcast_clamp_fusion), kind=kCustom, calls=%fused_computation | custom fusion | bytes 24576 | tf_op jit(solution)/shard_map/jit(_take)/gather | solution.py:136
  33.2 6.0 %all-to-all-start.2 = ((f32[2,8,256]{2,0,1:T(2,128)}), f32[2,8,256]{2,0,1:T(2,128)}, u32[]{:S(2)}, u32[]{:S(2)}) async-start(f32[2,8,256]{2,0,1:T(2,128)} %bitcast.15), calls=%async_computation.2 | async-start | bytes 32768 | tf_op jit(solution)/shard_map/all_to_all | solution.py:122
  41.3 0.9 pad_maximum_fusion.9
  42.2 3.9 %collective-permute-start = (f32[363,1,128]{2,1,0:T(1,128)}, f32[363,1,128]{2,1,0:T(1,128)S(1)}, u32[]{:S(2)}, u32[]{:S(2)}) collective-permute-start(f32[363,1,128]{2,1,0:T(1,128)} %get-tuple-element.15), channel_id=1, source_target_pairs={{0,4},{4,8},{8,12},{12,16},{16,20},{20,24},{24,28},{1,5},{5,9},{9,... | collective-permute-start | bytes 557576 | tf_op jit(solution)/shard_map/ppermute | solution.py:22
  46.2 1.3 %collective-permute-start.1 = (f32[363,1,128]{2,1,0:T(1,128)S(1)}, f32[363,1,128]{2,1,0:T(1,128)S(1)}, u32[]{:S(2)}, u32[]{:S(2)}) collective-permute-start(f32[363,1,128]{2,1,0:T(1,128)S(1)} %get-tuple-element.16), channel_id=1, source_target_pairs={{4,0},{8,4},{12,8},{16,12},{20,16},{24,20},{28,24},{5,1},{9,5},{13... | collective-permute-start | bytes 557576 | tf_op jit(solution)/shard_map/ppermute | solution.py:23
  47.5 2.1 %copy.21 = f32[2,8,256]{0,2,1:T(8,128)} copy(f32[2,8,256]{2,0,1:T(2,128)} %all-to-all-done.2) | data formatting | bytes 32768 | tf_op jit(solution)/shard_map/all_to_all | solution.py:122
  49.5 8.8 %gather_fusion.1 = f32[2048,2]{1,0:T(8,128)} fusion(f32[2,2048]{0,1:T(8,128)} %bitcast.64, s32[2048]{0:T(1024)S(1)} %broadcast_clamp_fusion), kind=kCustom, calls=%fused_computation.1 | custom fusion | bytes 40960 | tf_op jit(solution)/shard_map/jit(_take)/gather | solution.py:133
  58.3 1.6 %select_bitcast_fusion = f32[2,2048]{0,1:T(8,128)S(1)} fusion(f32[2048,2]{1,0:T(8,128)} %gather_fusion.1, pred[2048]{0:T(1024)(128)(4,1)} %compare_and_fusion), kind=kLoop, calls=%fused_computation.37 | loop fusion | flops 4096 | bytes 34816 | tf_op jit(solution)/shard_map/jit(_take)/select_n | solution.py:133
  59.9 0.9 slice_reduce_fusion.1
  60.9 0.9 multiply_add_fusion.1
  61.8 2.9 %fusion.4 = f32[9,36,16,129]{3,2,1,0:T(8,128)S(1)} fusion(f32[9,36,16,128]{3,2,1,0:T(8,128)S(1)} %copy-done, f32[9,36,16,128]{3,2,1,0:T(8,128)S(1)} %multiply_add_fusion.1, f32[16,129]{1,0:T(8,128)S(1)} %copy-done.7), kind=kLoop, calls=%fused_computation.10 | loop fusion | flops 5349888 | bytes 7991616 | tf_op jit(solution)/shard_map/mul | solution.py:39
  66.1 1.6 %fusion.7 = f32[9,36,17,128]{3,2,1,0:T(8,128)S(1)} fusion(f32[9,36,18,128]{3,2,1,0:T(8,128)S(1)} %bitcast.63, f32[9,36,18,128]{3,2,1,0:T(8,128)S(1)} %multiply_add_fusion, f32[17,128]{1,0:T(8,128)S(1)} %fusion.15), kind=kLoop, calls=%fused_computation.14 | loop fusion | flops 5640192 | bytes 14109184 | tf_op jit(solution)/shard_map/mul | solution.py:39
  67.8 2.7 %multiply_reduce_fusion.1 = (f32[9,16,128]{2,1,0:T(8,128)S(1)}, f32[16,128]{1,0:T(8,128)S(1)}, f32[9,36,16,128]{3,2,1,0:T(8,128)}) fusion(f32[9,16,128]{2,1,0:T(8,128)S(1)} %maximum_multiply_fusion, f32[36]{0:T(128)S(1)} %copy-done.13, f32[9,36,16,128]{3,2,1,0:T(8,128)S(1)} %copy-done, f32[9,36,16,129]{3,2,1,0:T(8,128)S(1)} %fusion.4, ...), kind=kLoop, calls=%fused_computation.31 | loop fusion | flops 7278592 | bytes 16089232 | tf_op jit(solution)/shard_map/reduce_sum | solution.py:68
  70.5 5.7 %psum.14 = f32[2048]{0:T(1024)S(1)} all-reduce(f32[2048]{0:T(1024)S(1)} %bitcast.81), channel_id=1, replica_groups=mesh['blk'=8,'dir'=4] {'dir'}, use_global_device_ids=true, to_apply=%region_1.2 | all-reduce | flops 2048 | bytes 16384 | tf_op jit(solution)/shard_map/psum | solution.py:55
  76.4 3.9 %multiply_reduce_fusion = (f32[9,16,128]{2,1,0:T(8,128)S(1)}, f32[9,36,16,128]{3,2,1,0:T(8,128)}) fusion(f32[36]{0:T(128)S(1)} %copy-done.15, f32[9,36,16,128]{3,2,1,0:T(8,128)} %get-tuple-element.14, f32[9,16,128]{2,1,0:T(8,128)S(1)} %broadcast_subtract_fusion, f32[36]{0:T(128)S(1)} %copy-done.14), kind=kLoop, calls=%fused_computation.30 | loop fusion | flops 3299328 | bytes 5456160 | tf_op jit(solution)/shard_map/reduce_sum | solution.py:69
  80.4 11.1 %psum.15 = f32[4,2048]{1,0:T(4,128)S(1)} all-reduce(f32[4,2048]{1,0:T(4,128)S(1)} %pad_maximum_fusion.10), channel_id=1, replica_groups=mesh['blk'=8,'dir'=4] {'dir'}, use_global_device_ids=true, to_apply=%region_8.9 | all-reduce | flops 8192 | bytes 65536 | tf_op jit(solution)/shard_map/psum | solution.py:143
  91.7 0.7 reduce.12
  92.5 12.9 %all_to_all.46 = f32[8,1,256]{2,1,0:T(1,128)S(1)} all-to-all(f32[8,1,256]{2,1,0:T(1,128)S(1)} %reshape.357), channel_id=1, replica_groups=mesh['blk'=8,'dir'=4] {'blk'}, dimensions={0} | all-to-all | bytes 16384 | tf_op jit(solution)/shard_map/all_to_all | solution.py:146
  (71 shorter events, 9.2 us)
Async XLA Ops:
  0.6 14.1 %all-to-all-start.1 = ((f32[1,8,256]{2,0,1:T(1,128)}), f32[1,8,256]{2,0,1:T(1,128)S(1)}, u32[]{:S(2)}, u32[]{:S(2)}) async-start(f32[1,8,256]{2,0,1:T(1,128)} %bitcast.89), calls=%async_computation.1 | async-start | bytes 16384 | tf_op jit(solution)/shard_map/all_to_all | solution.py:129
  14.7 18.4 %all-to-all-start = ((f32[8,1,512]{2,1,0:T(1,128)}), f32[8,1,512]{2,1,0:T(1,128)S(1)}, u32[]{:S(2)}, u32[]{:S(2)}) async-start(f32[8,1,512]{2,1,0:T(1,128)} %reshape.355), calls=%async_computation | async-start | bytes 32768 | tf_op jit(solution)/shard_map/all_to_all | solution.py:88
  20.7 11.8 %copy-start.2 = (s32[16,128]{1,0:T(8,128)S(1)}, s32[16,128]{1,0:T(8,128)}, u32[]{:S(2)}) copy-start(s32[16,128]{1,0:T(8,128)} %param.9) | copy-start | bytes 24580
  20.7 20.6 %copy-start = (f32[9,36,16,128]{3,2,1,0:T(8,128)S(1)}, f32[9,36,16,128]{3,2,1,0:T(8,128)}, u32[]{:S(2)}) copy-start(f32[9,36,16,128]{3,2,1,0:T(8,128)} %param.6) | copy-start | bytes 7962628
  20.8 20.6 %copy-start.1 = (f32[36,16,128]{2,1,0:T(8,128)S(1)}, f32[36,16,128]{2,1,0:T(8,128)}, u32[]{:S(2)}) copy-start(f32[36,16,128]{2,1,0:T(8,128)} %param.7) | copy-start | bytes 884740
  33.2 14.3 %all-to-all-start.2 = ((f32[2,8,256]{2,0,1:T(2,128)}), f32[2,8,256]{2,0,1:T(2,128)}, u32[]{:S(2)}, u32[]{:S(2)}) async-start(f32[2,8,256]{2,0,1:T(2,128)} %bitcast.15), calls=%async_computation.2 | async-start | bytes 32768 | tf_op jit(solution)/shard_map/all_to_all | solution.py:122
  42.2 22.7 %collective-permute-start = (f32[363,1,128]{2,1,0:T(1,128)}, f32[363,1,128]{2,1,0:T(1,128)S(1)}, u32[]{:S(2)}, u32[]{:S(2)}) collective-permute-start(f32[363,1,128]{2,1,0:T(1,128)} %get-tuple-element.15), channel_id=1, source_target_pairs={{0,4},{4,8},{8,12},{12,16},{16,20},{20,24},{24,28},{1,5},{5,9},{9,... | collective-permute-start | bytes 557576 | tf_op jit(solution)/shard_map/ppermute | solution.py:22
  46.2 18.7 %collective-permute-start.1 = (f32[363,1,128]{2,1,0:T(1,128)S(1)}, f32[363,1,128]{2,1,0:T(1,128)S(1)}, u32[]{:S(2)}, u32[]{:S(2)}) collective-permute-start(f32[363,1,128]{2,1,0:T(1,128)S(1)} %get-tuple-element.16), channel_id=1, source_target_pairs={{4,0},{8,4},{12,8},{16,12},{20,16},{24,20},{28,24},{5,1},{9,5},{13... | collective-permute-start | bytes 557576 | tf_op jit(solution)/shard_map/ppermute | solution.py:23
  58.3 2.5 %copy-start.8 = (f32[16,128]{1,0:T(8,128)S(1)}, f32[16,128]{1,0:T(8,128)}, u32[]{:S(2)}) copy-start(f32[16,128]{1,0:T(8,128)} %slice_bitcast_fusion) | copy-start | bytes 24580
  58.3 3.5 %copy-start.7 = (f32[16,129]{1,0:T(8,128)S(1)}, f32[16,129]{1,0:T(8,128)}, u32[]{:S(2)}) copy-start(f32[16,129]{1,0:T(8,128)} %fusion.13) | copy-start | bytes 24772
  60.8 3.9 %copy-start.3 = (f32[2048]{0:T(1024)}, f32[2048]{0:T(1024)S(1)}, u32[]{:S(2)}) copy-start(f32[2048]{0:T(1024)S(1)} %get-tuple-element.5) | copy-start | bytes 24580
  61.8 3.0 %copy-start.5 = (f32[16,128]{1,0:T(8,128)S(1)}, f32[16,128]{1,0:T(8,128)}, u32[]{:S(2)}) copy-start(f32[16,128]{1,0:T(8,128)} %fusion.17) | copy-start | bytes 24580
  61.8 3.0 %copy-start.9 = (f32[9]{0:T(128)S(1)}, f32[9]{0:T(128)}, u32[]{:S(2)}) copy-start(f32[9]{0:T(128)} %get-tuple-element.19) | copy-start | bytes 112
  61.8 3.0 %copy-start.11 = (f32[9]{0:T(128)S(1)}, f32[9]{0:T(128)}, u32[]{:S(2)}) copy-start(f32[9]{0:T(128)} %get-tuple-element.20) | copy-start | bytes 112
  66.1 1.6 %copy-start.13 = (f32[36]{0:T(128)S(1)}, f32[36]{0:T(128)}, u32[]{:S(2)}) copy-start(f32[36]{0:T(128)} %fusion.21) | copy-start | bytes 436
  67.7 8.5 %copy-start.4 = (f32[2048]{0:T(1024)S(1)}, f32[2048]{0:T(1024)}, u32[]{:S(2)}) copy-start(f32[2048]{0:T(1024)} %copy-done.3) | copy-start | bytes 24580
  67.7 8.5 %copy-start.6 = (f32[16,128]{1,0:T(8,128)S(1)}, f32[16,128]{1,0:T(8,128)}, u32[]{:S(2)}) copy-start(f32[16,128]{1,0:T(8,128)} %fusion.17) | copy-start | bytes 24580
  67.7 8.5 %copy-start.10 = (f32[9]{0:T(128)S(1)}, f32[9]{0:T(128)}, u32[]{:S(2)}) copy-start(f32[9]{0:T(128)} %get-tuple-element.19) | copy-start | bytes 112
  67.7 8.5 %copy-start.12 = (f32[9]{0:T(128)S(1)}, f32[9]{0:T(128)}, u32[]{:S(2)}) copy-start(f32[9]{0:T(128)} %get-tuple-element.20) | copy-start | bytes 112
  67.7 8.6 %copy-start.14 = (f32[36]{0:T(128)S(1)}, f32[36]{0:T(128)}, u32[]{:S(2)}) copy-start(f32[36]{0:T(128)} %get-tuple-element.21) | copy-start | bytes 436
  67.8 8.6 %copy-start.15 = (f32[36]{0:T(128)S(1)}, f32[36]{0:T(128)}, u32[]{:S(2)}) copy-start(f32[36]{0:T(128)} %get-tuple-element.22) | copy-start | bytes 436
where the time goes:
time: 108 us; the launch traced here: 107 us
  blocking collectives  29.8 us (28%)
  local copies, waits for them, and re-layouts  28 us (26%)
  starting transfers between devices  24.5 us (23%)
  other arithmetic  23.7 us (22%)
  between operations  1.13 us (1%)
    all_to_all x1, blocking collectives, on_device(): lax.all_to_all(ocean_grid, 'blk', split_axis=1, concat_axis=2, tiled=True)  12.9 us
    gather x1, local copies, waits for them, and re-layouts, on_device(): jnp.take(ice_back.reshape(1, cell_count), slot_index, axis=1, mode='fill'...  11.8 us
    psum x1, blocking collectives, on_device(): summed = lax.psum(partial_geo, 'dir')  11.1 us
    gather x1, local copies, waits for them, and re-layouts, on_device(): jnp.take(wind_back.reshape(2, cell_count), slot_index, axis=1, mode='fill...  8.8 us
    all_to_all x1, starting transfers between devices, on_device(): lax.all_to_all(ice_cover.reshape(1, blocks, capacity), 'blk', split_axis=...  7.29 us
    all_to_all x1, starting transfers between devices, on_device(): lax.all_to_all(ocean_current, 'blk', split_axis=2, concat_axis=1, tiled=T...  6 us
    all_to_all x1, starting transfers between devices, on_device(): lax.all_to_all(wind_vector[0].reshape(2, blocks, capacity), 'blk', split_...  5.98 us
    psum x1, blocking collectives, source_terms(): moment = lax.psum(moment_band, 'dir')  5.73 us
  transfers between devices with their start and end apart: 5, of which 0 were waited for; matrix products, arithmetic and copies ran while one was open for 37% of the time, Pallas kernels for 0%

commit v1 on v0

v1 whole, which is shorter than its diff:
```python
import functools
import math

import jax
import jax.numpy as jnp
import numpy as np
from jax import lax
from jax.experimental import pallas as pl
from jax.experimental.pallas import tpu as pltpu
from jax.sharding import PartitionSpec as P

COURANT = 0.15
WIND_GROWTH = 0.15
DAMP_RATE = 0.5
STEEP_COEF = 0.01
STRESS_SCALE = 1.0
STOKES_SCALE = 0.15
RATIO_STEP = 1.1
LANES = 128
MESH = pl.DeviceIdType.MESH


def moved_and_sums(
    shape,
    trig_ref, ratio_ref, spec_hbm, speed_ref, ocean_ref, route_ref, wind_ref, ice_ref,
    moved_hbm, gain_ref, damp_ref, force_ref,
    spec, moved, face_x, face_y, edge_out, edge_in, side_out, side_in,
    ocean_in, ocean_yx, ocean_xy, wind_in, ice_in, table, sums, part, part_in, stage, force_in,
    load_sem, store_sem, edge_send, edge_recv, side_send, side_recv,
    ocean_send, ocean_recv, wind_send, wind_recv, ice_send, ice_recv,
    part_send, part_recv, force_send, force_recv,
):
    blocks, bands, dirs, freqs, rows, yrows, chunk = shape
    width = rows * freqs
    b = lax.axis_index("blk")
    d = lax.axis_index("dir")
    capacity = rows * LANES // blocks
    wide = max(capacity, LANES)
    tiles = wide // LANES
    chunks = dirs // chunk

    def load(j):
        return pltpu.make_async_copy(spec_hbm.at[j], spec.at[j], load_sem.at[j])

    for j in range(dirs):
        load(j).start()

    barrier = pltpu.get_barrier_semaphore()

    def greet_blk(o, carry):
        pl.semaphore_signal(
            barrier, inc=1, device_id=(lax.rem(b + o, blocks), d), device_id_type=MESH
        )
        return carry

    lax.fori_loop(1, blocks, greet_blk, 0)
    for o in range(1, bands):
        pl.semaphore_signal(
            barrier, inc=1, device_id=(b, lax.rem(d + o, bands)), device_id_type=MESH
        )

    sea = jnp.where(route_ref[...] >= 0, 1.0, 0.0).astype(jnp.float32)
    for side, row in ((0, rows - 1), (1, 0)):
        side_out[side, :freqs, :] = speed_ref[pl.ds(row, freqs, stride=rows), :]
        side_out[side, freqs : freqs + 1, :] = sea[row : row + 1, :]

    @pl.when(b == 0)
    def _():
        side_in[0] = jnp.zeros_like(side_in[0])
        edge_in[0] = jnp.zeros_like(edge_in[0])

    @pl.when(b == blocks - 1)
    def _():
        side_in[1] = jnp.zeros_like(side_in[1])
        edge_in[1] = jnp.zeros_like(edge_in[1])

    pl.semaphore_wait(barrier, blocks - 1 + bands - 1)

    def ocean_copy(to, src, slot):
        return pltpu.make_async_remote_copy(
            src_ref=ocean_ref, dst_ref=ocean_in.at[src], send_sem=ocean_send.at[slot],
            recv_sem=ocean_recv.at[src], device_id=(to, d), device_id_type=MESH,
        )

    def wind_copy(to, src, slot):
        start = pl.multiple_of(((to * capacity) // LANES) * LANES, LANES)
        return pltpu.make_async_remote_copy(
            src_ref=wind_ref.at[0, :, pl.ds(start, wide)], dst_ref=wind_in.at[src],
            send_sem=wind_send.at[slot], recv_sem=wind_recv.at[src],
            device_id=(to, d), device_id_type=MESH,
        )

    def ice_copy(to, src, slot):
        start = pl.multiple_of(((to * capacity) // LANES) * LANES, LANES)
        return pltpu.make_async_remote_copy(
            src_ref=ice_ref.at[:, pl.ds(start, wide)], dst_ref=ice_in.at[src],
            send_sem=ice_send.at[slot], recv_sem=ice_recv.at[src],
            device_id=(to, d), device_id_type=MESH,
        )

    def send_ocean(o, carry):
        ocean_copy(lax.rem(b + o, blocks), b, o).start()
        return carry

    def send_winds(o, carry):
        to = lax.rem(b + o, blocks)
        wind_copy(to, b, o).start()
        ice_copy(to, b, o).start()
        return carry

    lax.fori_loop(1, blocks, send_ocean, 0)

    def side_copy(side):
        return pltpu.make_async_remote_copy(
            src_ref=side_out.at[side], dst_ref=side_in.at[side], send_sem=side_send.at[side],
            recv_sem=side_recv.at[side], device_id=(b + 1 - 2 * side, d), device_id_type=MESH,
        )

    def edge_copy(side, c):
        part_of = pl.ds(c * chunk, chunk)
        return pltpu.make_async_remote_copy(
            src_ref=edge_out.at[side, part_of], dst_ref=edge_in.at[side, part_of],
            send_sem=edge_send.at[side, c], recv_sem=edge_recv.at[side, c],
            device_id=(b + 1 - 2 * side, d), device_id_type=MESH,
        )

    sends = ((0, b < blocks - 1), (1, b > 0))
    receives = ((0, b > 0), (1, b < blocks - 1))
    for side, has in sends:
        @pl.when(has)
        def _(side=side):
            side_copy(side).start()

    for c in range(chunks):
        for j in range(c * chunk, (c + 1) * chunk):
            load(j).wait()
            for side, row in ((0, rows - 1), (1, 0)):
                edge_out[side, j] = spec[j, pl.ds(row, freqs, stride=rows), :]
        for side, has in sends:
            @pl.when(has)
            def _(side=side, c=c):
                edge_copy(side, c).start()

    lax.fori_loop(1, blocks, send_winds, 0)

    row_id = lax.broadcasted_iota(jnp.int32, (rows, LANES), 0)
    lane_id = lax.broadcasted_iota(jnp.int32, (rows, LANES), 1)

    def next_row(value):
        return pltpu.roll(value, rows - 1, 0)

    def next_lane(value):
        return pltpu.roll(value, LANES - 1, 1)

    half = 0.5 * COURANT
    open_x = jnp.where(row_id < rows - 1, half * sea * next_row(sea), 0.0)
    open_y = jnp.where(lane_id < LANES - 1, half * sea * next_lane(sea), 0.0)

    def faces(k, carry):
        at = pl.ds(pl.multiple_of(k * rows, rows), rows)
        speed = speed_ref[at, :]
        face_x[at, :] = open_x * (speed + next_row(speed))
        face_y[at, :] = open_y * (speed + next_lane(speed))
        return carry

    lax.fori_loop(0, freqs, faces, 0, unroll=4)

    ocean_in[b] = ocean_ref[...]

    def wait_ocean(o, carry):
        ocean_copy(lax.rem(b + o, blocks), lax.rem(b + o, blocks), o).wait_recv()
        return carry

    lax.fori_loop(1, blocks, wait_ocean, 0)

    def lay_ocean(i, carry):
        at = i * yrows
        if yrows % 8 == 0:
            at = pl.multiple_of(at, 8)
        for comp in range(2):
            ocean_yx[comp, pl.ds(at, yrows), :] = ocean_in[i, comp]
        return carry

    lax.fori_loop(0, blocks, lay_ocean, 0)
    ocean_xy[:, 0:8, :] = jnp.zeros((2, 8, LANES), jnp.float32)
    total = blocks * rows
    ocean_xy[:, total + 8 : total + 16, :] = jnp.zeros((2, 8, LANES), jnp.float32)
    for comp in range(2):
        for t in range(total // LANES):
            ocean_xy[comp, 8 + t * LANES : 8 + (t + 1) * LANES, :] = jnp.transpose(
                ocean_yx[comp, :, t * LANES : (t + 1) * LANES]
            )
    own = pl.ds(pl.multiple_of(b * rows + 8, 8), rows)
    flow_x = ocean_xy[0, own, :]
    flow_y = ocean_xy[1, own, :]
    flow_low = ocean_xy[0, pl.ds(b * rows + 7, 1), :]
    flow_high = ocean_xy[0, pl.ds(b * rows + 8 + rows, 1), :]
    cur_x = open_x * (flow_x + next_row(flow_x))
    cur_y = open_y * (flow_y + next_lane(flow_y))

    group = 1
    for size in (6, 5, 4, 3, 2):
        if freqs % size == 0:
            group = size
            break

    def one_dir(j, carry):
        cosine = trig_ref[0, d * dirs + j]
        sine = trig_ref[1, d * dirs + j]

        def some_freqs(g, acc):
            two, three, four = acc
            for i in range(group):
                k = g * group + i
                at = pl.ds(pl.multiple_of(k * rows, rows), rows)
                energy = spec[j, at, :]
                speed_x = face_x[at, :] * cosine + cur_x
                flux_x = speed_x * jnp.where(speed_x > 0.0, energy, next_row(energy))
                speed_y = face_y[at, :] * sine + cur_y
                flux_y = speed_y * jnp.where(speed_y > 0.0, energy, next_lane(energy))
                value = (
                    sea * energy - (flux_x - pltpu.roll(flux_x, 1, 0))
                ) - (flux_y - pltpu.roll(flux_y, 1, 1))
                moved[j, at, :] = value
                two = two + ratio_ref[0, k] * value
                three = three + ratio_ref[1, k] * value
                four = four + ratio_ref[2, k] * value
            return two, three, four

        zero = jnp.zeros((rows, LANES), jnp.float32)
        acc = lax.fori_loop(0, freqs // group, some_freqs, (zero, zero, zero))
        for i in range(3):
            sums[j, i] = acc[i]
        return carry

    lax.fori_loop(0, dirs, one_dir, 0)

    high = blocks * tiles
    own_lane = pl.multiple_of(((b * capacity) // LANES) * LANES, LANES)
    wind_in[b] = wind_ref[0, :, pl.ds(own_lane, wide)]
    ice_in[b] = ice_ref[:, pl.ds(own_lane, wide)]

    def wait_winds(o, carry):
        src = lax.rem(b + o, blocks)
        wind_copy(src, src, o).wait_recv()
        ice_copy(src, src, o).wait_recv()
        return carry

    lax.fori_loop(1, blocks, wait_winds, 0)

    def lay_table(i, carry):
        for t in range(tiles):
            lanes = slice(t * LANES, (t + 1) * LANES)
            for comp in range(2):
                table[pl.ds(comp * high + i * tiles + t, 1), :] = wind_in[i, comp : comp + 1, lanes]
            table[pl.ds(2 * high + i * tiles + t, 1), :] = ice_in[i, :, lanes]
        return carry

    lax.fori_loop(0, blocks, lay_table, 0)
    whole = table[...]
    first = whole.astype(jnp.bfloat16)
    rest = whole - first.astype(jnp.float32)
    second = rest.astype(jnp.bfloat16)
    third = (rest - second.astype(jnp.float32)).astype(jnp.bfloat16)
    entry_id = lax.broadcasted_iota(jnp.int32, (LANES, LANES), 0)
    high_id = lax.broadcasted_iota(jnp.int32, (high, LANES), 0)
    per_row = int(math.log2(min(capacity, LANES)))
    offset = lax.rem(b * capacity, LANES) if capacity < LANES else 0
    found = [[], [], []]
    for row in range(rows):
        slot = route_ref[row : row + 1, :]
        upper = lax.shift_right_arithmetic(slot, per_row)
        lower = jnp.bitwise_and(slot, (1 << per_row) - 1) + offset
        hot = jnp.where(entry_id == lower, 1.0, 0.0).astype(jnp.bfloat16)
        values = sum(
            jnp.dot(piece, hot, preferred_element_type=jnp.float32)
            for piece in (third, second, first)
        )
        here = high_id == upper
        for i in range(3):
            found[i].append(
                jnp.sum(
                    jnp.where(here, values[i * high : (i + 1) * high], 0.0), axis=0, keepdims=True
                )
            )
    wind_x, wind_y, ice = (jnp.concatenate(value, axis=0) for value in found)
    growth = WIND_GROWTH * (1.0 - ice)

    for side, has in receives:
        @pl.when(has)
        def _(side=side):
            side_copy(side).wait_recv()
    low_open = half * side_in[0, freqs : freqs + 1, :] * sea[0:1]
    high_open = half * side_in[1, freqs : freqs + 1, :] * sea[rows - 1 : rows]
    low_face = low_open * (side_in[0, :freqs, :] + side_out[1, :freqs, :])
    high_face = high_open * (side_in[1, :freqs, :] + side_out[0, :freqs, :])
    low_cur = low_open * (flow_low + flow_x[0:1])
    high_cur = high_open * (flow_high + flow_x[rows - 1 : rows])
    power = lax.broadcasted_iota(jnp.int32, (freqs, LANES), 0).astype(jnp.float32) - (freqs - 1)
    ratio = jnp.exp(power * math.log(RATIO_STEP))
    square = ratio * ratio
    weights = (square, square * ratio, square * square)

    zero = jnp.zeros((rows, LANES), jnp.float32)
    moment, stress_x, stress_y, base_x, base_y, damp_x, damp_y = [zero] * 7
    for c in range(chunks):
        for side, has in receives:
            @pl.when(has)
            def _(side=side, c=c):
                edge_copy(side, c).wait_recv()
        for j in range(c * chunk, (c + 1) * chunk):
            cosine = trig_ref[0, d * dirs + j]
            sine = trig_ref[1, d * dirs + j]
            low_speed = low_face * cosine + low_cur
            high_speed = high_face * cosine + high_cur
            low_flux = low_speed * jnp.where(low_speed > 0.0, edge_in[0, j], edge_out[1, j])
            high_flux = high_speed * jnp.where(high_speed > 0.0, edge_out[0, j], edge_in[1, j])
            low_at = pl.ds(0, freqs, stride=rows)
            high_at = pl.ds(rows - 1, freqs, stride=rows)
            moved[j, low_at, :] = moved[j, low_at, :] + low_flux
            moved[j, high_at, :] = moved[j, high_at, :] - high_flux
            pltpu.make_async_copy(moved.at[j], moved_hbm.at[j], store_sem.at[j]).start()
            fixed = []
            for i in range(3):
                low_sum = jnp.sum(weights[i] * low_flux, axis=0, keepdims=True)
                high_sum = jnp.sum(weights[i] * high_flux, axis=0, keepdims=True)
                fixed.append(
                    sums[j, i]
                    + jnp.where(row_id == 0, low_sum, 0.0)
                    - jnp.where(row_id == rows - 1, high_sum, 0.0)
                )
            two, three, four = fixed
            gain = growth * jnp.maximum(wind_x * cosine + wind_y * sine, 0.0)
            gain_ref[j] = gain
            moment = moment + two
            stress = gain * two
            stress_x = stress_x + cosine * stress
            stress_y = stress_y + sine * stress
            base = three + gain * four
            base_x = base_x + cosine * base
            base_y = base_y + sine * base
            damp_x = damp_x + cosine * four
            damp_y = damp_y + sine * four

    pairs = (
        (STRESS_SCALE * stress_x, zero),
        (STRESS_SCALE * stress_y, zero),
        (STOKES_SCALE * base_x, STOKES_SCALE * damp_x),
        (STOKES_SCALE * base_y, STOKES_SCALE * damp_y),
    )
    for comp in range(4):
        part[comp, 0] = moment
        part[comp, 1] = pairs[comp][0]
        part[comp, 2] = pairs[comp][1]

    def part_copy(to, src, slot):
        return pltpu.make_async_remote_copy(
            src_ref=part.at[to], dst_ref=part_in.at[src], send_sem=part_send.at[slot],
            recv_sem=part_recv.at[src], device_id=(b, to), device_id_type=MESH,
        )

    for o in range(1, bands):
        part_copy(lax.rem(d + o, bands), d, o).start()
    part_in[d] = part[d]
    for o in range(1, bands):
        src = lax.rem(d + o, bands)
        part_copy(src, src, o).wait_recv()
    summed = part_in[0]
    for i in range(1, bands):
        summed = summed + part_in[i]
    steepness = STEEP_COEF * summed[0]
    damping = DAMP_RATE * steepness / (1.0 + steepness)
    damp_ref[...] = damping
    force = summed[1] - damping * summed[2]

    square_tile = jnp.concatenate([force, jnp.zeros((LANES - rows, LANES), jnp.float32)], axis=0)
    per_tile = LANES // rows
    stage[...] = jnp.transpose(
        pltpu.roll(square_tile, lax.rem(b, per_tile) * rows, 0)
    )
    if yrows % 8 == 0:
        def force_src(i):
            return stage.at[pl.ds(pl.multiple_of(i * yrows, 8), yrows)]
    else:
        def force_src(i):
            return force_in.at[blocks + i]

        def lay_force(i, carry):
            force_in[blocks + i] = stage[pl.ds(i * yrows, yrows), :]
            return carry

        lax.fori_loop(0, blocks, lay_force, 0)

    def force_copy(to, src, slot):
        return pltpu.make_async_remote_copy(
            src_ref=force_src(to), dst_ref=force_in.at[src], send_sem=force_send.at[slot],
            recv_sem=force_recv.at[src], device_id=(to, d), device_id_type=MESH,
        )

    def send_force(o, carry):
        force_copy(lax.rem(b + o, blocks), b, o).start()
        return carry

    def wait_force(o, carry):
        src = lax.rem(b + o, blocks)
        force_copy(src, src, o).wait_recv()
        return carry

    lax.fori_loop(1, blocks, send_force, 0)
    force_in[b] = stage[pl.ds(b * yrows if yrows % 8 else pl.multiple_of(b * yrows, 8), yrows), :]

    def drain(o, carry):
        to = lax.rem(b + o, blocks)
        ocean_copy(to, b, o).wait_send()
        wind_copy(to, b, o).wait_send()
        ice_copy(to, b, o).wait_send()
        return carry

    lax.fori_loop(1, blocks, drain, 0)
    for side, has in sends:
        @pl.when(has)
        def _(side=side):
            side_copy(side).wait_send()
            for c in range(chunks):
                edge_copy(side, c).wait_send()
    for o in range(1, bands):
        part_copy(lax.rem(d + o, bands), d, o).wait_send()
    for j in range(dirs):
        pltpu.make_async_copy(moved.at[j], moved_hbm.at[j], store_sem.at[j]).wait()

    lax.fori_loop(1, blocks, wait_force, 0)
    for t in range(blocks // per_tile):
        tile = force_in[t * per_tile]
        for i in range(1, per_tile):
            tile = tile + force_in[t * per_tile + i]
        force_ref[0, :, t * LANES : (t + 1) * LANES] = tile

    def drain_force(o, carry):
        force_copy(lax.rem(b + o, blocks), b, o).wait_send()
        return carry

    lax.fori_loop(1, blocks, drain_force, 0)


def on_device(spectrum, group_speed, ocean_current, route_slot, wind_vector, ice_cover):
    blocks = lax.axis_size("blk")
    bands = lax.axis_size("dir")
    dirs, freqs, rows, width = spectrum.shape
    yrows = ocean_current.shape[1]
    capacity = rows * width // blocks
    wide = max(capacity, LANES)
    chunk = 3 if dirs % 3 == 0 else 1
    chunks = dirs // chunk
    high = blocks * (wide // LANES)
    total = blocks * rows
    padded = (freqs // 8 + 1) * 8
    f32 = jnp.float32
    count = dirs * bands
    angles = 2.0 * np.pi * np.arange(count) / count
    trig = jnp.asarray(np.stack([np.cos(angles), np.sin(angles)]), f32)
    ratios = RATIO_STEP ** (np.arange(freqs) - (freqs - 1.0))
    ratio_table = jnp.asarray(np.stack([ratios**2, ratios**3, ratios**4]), f32)
    shape = (blocks, bands, dirs, freqs, rows, yrows, chunk)
    vmem = pl.BlockSpec(memory_space=pltpu.VMEM)
    smem = pl.BlockSpec(memory_space=pltpu.SMEM)
    anywhere = pl.BlockSpec(memory_space=pl.ANY)
    dma = pltpu.SemaphoreType.DMA
    force_slots = blocks if yrows % 8 == 0 else 2 * blocks
    moved, gain, damping, forcing = pl.pallas_call(
        functools.partial(moved_and_sums, shape),
        out_shape=(
            jax.ShapeDtypeStruct((dirs, freqs * rows, width), f32),
            jax.ShapeDtypeStruct((dirs, rows, width), f32),
            jax.ShapeDtypeStruct((rows, width), f32),
            jax.ShapeDtypeStruct((1, yrows, total), f32),
        ),
        in_specs=[smem, smem, anywhere, vmem, vmem, vmem, vmem, vmem],
        out_specs=(anywhere, vmem, vmem, vmem),
        scratch_shapes=[
            pltpu.VMEM((dirs, freqs * rows, width), f32),
            pltpu.VMEM((dirs, freqs * rows, width), f32),
            pltpu.VMEM((freqs * rows, width), f32),
            pltpu.VMEM((freqs * rows, width), f32),
            pltpu.VMEM((2, dirs, freqs, width), f32),
            pltpu.VMEM((2, dirs, freqs, width), f32),
            pltpu.VMEM((2, padded, width), f32),
            pltpu.VMEM((2, padded, width), f32),
            pltpu.VMEM((blocks, 2, yrows, total), f32),
            pltpu.VMEM((2, blocks * yrows, total), f32),
            pltpu.VMEM((2, total + 16, width), f32),
            pltpu.VMEM((blocks, 2, wide), f32),
            pltpu.VMEM((blocks, 1, wide), f32),
            pltpu.VMEM((3 * high, LANES), f32),
            pltpu.VMEM((dirs, 3, rows, width), f32),
            pltpu.VMEM((4, 3, rows, width), f32),
            pltpu.VMEM((bands, 3, rows, width), f32),
            pltpu.VMEM((width, LANES), f32),
            pltpu.VMEM((force_slots, yrows, LANES), f32),
            dma((dirs,)), dma((dirs,)),
            dma((2, chunks)), dma((2, chunks)), dma((2,)), dma((2,)),
            dma((blocks,)), dma((blocks,)), dma((blocks,)), dma((blocks,)),
            dma((blocks,)), dma((blocks,)),
            dma((bands,)), dma((bands,)), dma((blocks,)), dma((blocks,)),
        ],
        compiler_params=pltpu.CompilerParams(
            collective_id=0, has_side_effects=True, vmem_limit_bytes=48 * 1024 * 1024
        ),
        cost_estimate=pl.CostEstimate(
            flops=30 * spectrum.size, bytes_accessed=8 * spectrum.size, transcendentals=0
        ),
    )(
        trig, ratio_table, spectrum.reshape(dirs, freqs * rows, width),
        group_speed.reshape(freqs * rows, width), ocean_current, route_slot, wind_vector, ice_cover,
    )
    growth = jnp.asarray(ratios, f32)[None, :, None, None] * (gain - damping)[:, None]
    result = moved.reshape(dirs, freqs, rows, width) * (1.0 + growth)
    return result, forcing


def solution(mesh):
    return jax.shard_map(
        on_device,
        mesh=mesh,
        in_specs=(
            P("dir", None, "blk", None),
            P(None, "blk", None),
            P(None, "blk", None),
            P("blk", None),
            P("blk", None, None),
            P("blk", None),
        ),
        out_specs=(P("dir", None, "blk", None), P("dir", "blk", None)),
        check_vma=False,
    )
```

time: 108 us -> 42 us (0.39)
  Pallas kernels: 0 us -> 31.5 us
  blocking collectives: 29.8 us -> 0 us
  starting transfers between devices: 24.5 us -> 0 us
  other arithmetic: 23.7 us -> 1.87 us
  local copies, waits for them, and re-layouts: 28 us -> 7.5 us
    pallas_call x0 -> x1, Pallas kernels: none -> 31.5 us  [on_device(): pl.pallas_call(functools.partial(moved_and_sums, shape), out_shape=(jax.S...]
    gather x2 -> x0, local copies, waits for them, and re-layouts: 20.6 us -> none  [the longest x1 11.8 us: on_device(): jnp.take(ice_back.reshape(1, cell_count), slot_index, axis=1, mode='fill'...]
    all_to_all x3 -> x0, starting transfers between devices: 19.3 us -> none  [the longest x1 7.29 us: on_device(): lax.all_to_all(ice_cover.reshape(1, blocks, capacity), 'blk', split_axis=...]
    psum x2 -> x0, blocking collectives: 16.8 us -> none  [the longest x1 11.1 us: on_device(): summed = lax.psum(partial_geo, 'dir')]
    all_to_all x1 -> x0, blocking collectives: 12.9 us -> none  [on_device(): lax.all_to_all(ocean_grid, 'blk', split_axis=1, concat_axis=2, tiled=True)]
    reduce_sum x3 -> x0, other arithmetic: 6.68 us -> none  [the longest x1 3.87 us: source_terms(): stokes_dir = jnp.sum(ratio_cube[None, :, None] * updated, axis=1)]
    unnamed x37 -> x19, local copies, waits for them, and re-layouts: 2.16 us -> 7.5 us
    ppermute x2 -> x0, starting transfers between devices: 5.22 us -> none  [the longest x1 3.92 us: with_halo(): before = lax.ppermute(last, axis, up)]
  transfers between devices with their start and end apart: 5 -> 0, of which waited for: 0 -> 0; matrix products, arithmetic and copies ran while one was open for 37% -> 0% of each run, Pallas kernels for 0% -> 0%
where the time goes in v1:
time: 42 us; the launch traced here: 41.5 us
  Pallas kernels  31.5 us (75%)
  local copies, waits for them, and re-layouts  7.5 us (18%)
  other arithmetic  1.87 us (4%)
  between operations  0.68 us (2%)
    pallas_call x1, Pallas kernels, on_device(): pl.pallas_call(functools.partial(moved_and_sums, shape), out_shape=(jax.S...  31.5 us
    unnamed x19, local copies, waits for them, and re-layouts  7.5 us
    mul x1, other arithmetic, on_device(): result = moved.reshape(dirs, freqs, rows, width) * (1.0 + growth)  1.86 us

profile of v1, /device:TPU:0, one launch (start us, length us, event | category | flops | bytes accessed | tf_op | source)
XLA Modules:
  0.0 41.5 jit_solution(7298257776338341732)
XLA Ops:
  0.6 0.0 copy-start.8
  0.6 0.0 copy-start
  0.7 1.7 %copy-done = f32[9,36,16,128]{3,2,1,0:T(8,128)S(1)} copy-done((f32[9,36,16,128]{3,2,1,0:T(8,128)S(1)}, f32[9,36,16,128]{3,2,1,0:T(8,128)}, u32[]{:S(2)}) %copy-start) | copy-done | bytes 2654232
  2.4 0.0 copy-start.1
  2.4 1.0 %copy-done.1 = f32[36,16,128]{2,1,0:T(8,128)S(1)} copy-done((f32[36,16,128]{2,1,0:T(8,128)S(1)}, f32[36,16,128]{2,1,0:T(8,128)}, u32[]{:S(2)}) %copy-start.1) | copy-done | bytes 294936
  3.4 0.0 copy-start.2
  3.4 0.7 %copy-done.2 = f32[2,16,128]{2,1,0:T(8,128)S(1)} copy-done((f32[2,16,128]{2,1,0:T(8,128)S(1)}, f32[2,16,128]{2,1,0:T(8,128)}, u32[]{:S(2)}) %copy-start.2) | copy-done | bytes 16408
  4.1 0.0 copy-start.3
  4.1 0.7 %copy-done.3 = f32[1,2,2048]{2,1,0:T(2,128)S(1)} copy-done((f32[1,2,2048]{2,1,0:T(2,128)S(1)}, f32[1,2,2048]{2,1,0:T(2,128)}, u32[]{:S(2)}) %copy-start.3) | copy-done | bytes 16408
  4.8 0.0 copy-start.4
  4.8 0.7 %copy-done.4 = s32[16,128]{1,0:T(8,128)S(1)} copy-done((s32[16,128]{1,0:T(8,128)S(1)}, s32[16,128]{1,0:T(8,128)}, u32[]{:S(2)}) %copy-start.4) | copy-done | bytes 8216
  5.5 0.0 copy-start.5
  5.5 0.7 %copy-done.5 = f32[1,2048]{1,0:T(1,128)S(1)} copy-done((f32[1,2048]{1,0:T(1,128)S(1)}, f32[1,2048]{1,0:T(1,128)}, u32[]{:S(2)}) %copy-start.5) | copy-done | bytes 8216
  6.2 0.0 copy-start.6
  6.2 0.7 %copy-done.6 = f32[3,36]{1,0:T(4,128)S(1)} copy-done((f32[3,36]{1,0:T(4,128)S(1)}, f32[3,36]{1,0:T(4,128)}, u32[]{:S(2)}) %copy-start.6) | copy-done | bytes 456
  6.9 0.0 copy-start.7
  6.9 0.7 %copy-done.7 = f32[2,36]{1,0:T(2,128)S(1)} copy-done((f32[2,36]{1,0:T(2,128)S(1)}, f32[2,36]{1,0:T(2,128)}, u32[]{:S(2)}) %copy-start.7) | copy-done | bytes 312
  7.6 31.5 %shard_map.104 = (f32[9,576,128]{2,1,0:T(8,128)S(1)}, f32[9,16,128]{2,1,0:T(8,128)S(1)}, f32[16,128]{1,0:T(8,128)S(1)}, f32[1,16,128]{2,1,0:T(8,128)S(1)}) custom-call(f32[2,36]{1,0:T(2,128)S(1)} %copy-done.7, f32[3,36]{1,0:T(4,128)S(1)} %copy-done.6, f32[9,576,128]{2,1,0:T(8,128)S(1)} %bitcast.3, f32[576,128]{1,0:T(8,128)S(1)} %bitcast.5, ...), custom_call_target="tpu_custom_call" | custom-call | flops 19906560 | bytes 5308416 | tf_op jit(solution)/shard_map/pallas_call | solution.py:469
  39.0 0.0 copy-done.8
  39.0 1.9 %add_multiply_fusion = f32[9,36,16,128]{3,2,1,0:T(8,128)} fusion(f32[9,36,16,128]{3,2,1,0:T(8,128)S(1)} %bitcast.4, f32[9,16,128]{2,1,0:T(8,128)S(1)} %broadcast_subtract_fusion, f32[36]{0:T(128)S(1)} %copy-done.8), kind=kLoop, calls=%fused_computation | loop fusion | flops 1990656 | bytes 5382288 | tf_op jit(solution)/shard_map/mul | solution.py:516
  40.9 0.6 %copy.12 = f32[1,16,128]{2,1,0:T(8,128)} copy(f32[1,16,128]{2,1,0:T(8,128)S(1)} %get-tuple-element.13) | data formatting | bytes 16384
  (1 shorter events, 0.0 us)
Async XLA Ops:
  0.6 38.4 %copy-start.8 = (f32[36]{0:T(128)S(1)}, f32[36]{0:T(128)}, u32[]{:S(2)}) copy-start(f32[36]{0:T(128)} %constant.10.clone) | copy-start | bytes 436
  0.6 1.8 %copy-start = (f32[9,36,16,128]{3,2,1,0:T(8,128)S(1)}, f32[9,36,16,128]{3,2,1,0:T(8,128)}, u32[]{:S(2)}) copy-start(f32[9,36,16,128]{3,2,1,0:T(8,128)} %param.9) | copy-start | bytes 7962628
  2.4 1.0 %copy-start.1 = (f32[36,16,128]{2,1,0:T(8,128)S(1)}, f32[36,16,128]{2,1,0:T(8,128)}, u32[]{:S(2)}) copy-start(f32[36,16,128]{2,1,0:T(8,128)} %param.10) | copy-start | bytes 884740
  3.4 0.7 %copy-start.2 = (f32[2,16,128]{2,1,0:T(8,128)S(1)}, f32[2,16,128]{2,1,0:T(8,128)}, u32[]{:S(2)}) copy-start(f32[2,16,128]{2,1,0:T(8,128)} %ocean_ref.1) | copy-start | bytes 49156
  4.1 0.7 %copy-start.3 = (f32[1,2,2048]{2,1,0:T(2,128)S(1)}, f32[1,2,2048]{2,1,0:T(2,128)}, u32[]{:S(2)}) copy-start(f32[1,2,2048]{2,1,0:T(2,128)} %wind_ref.1) | copy-start | bytes 49156
  4.8 0.7 %copy-start.4 = (s32[16,128]{1,0:T(8,128)S(1)}, s32[16,128]{1,0:T(8,128)}, u32[]{:S(2)}) copy-start(s32[16,128]{1,0:T(8,128)} %route_ref.1) | copy-start | bytes 24580
  5.5 0.7 %copy-start.5 = (f32[1,2048]{1,0:T(1,128)S(1)}, f32[1,2048]{1,0:T(1,128)}, u32[]{:S(2)}) copy-start(f32[1,2048]{1,0:T(1,128)} %ice_ref.1) | copy-start | bytes 24580
  6.2 0.7 %copy-start.6 = (f32[3,36]{1,0:T(4,128)S(1)}, f32[3,36]{1,0:T(4,128)}, u32[]{:S(2)}) copy-start(f32[3,36]{1,0:T(4,128)} %constant.9.clone.ratio_ref) | copy-start | bytes 1300
  6.9 0.7 %copy-start.7 = (f32[2,36]{1,0:T(2,128)S(1)}, f32[2,36]{1,0:T(2,128)}, u32[]{:S(2)}) copy-start(f32[2,36]{1,0:T(2,128)} %constant.8.clone.trig_ref) | copy-start | bytes 868

commit v2 on v1

--- a/solution.py
+++ b/solution.py
@@ -22,11 +22,12 @@
 
 def moved_and_sums(
     shape,
-    trig_ref, ratio_ref, spec_hbm, speed_ref, ocean_ref, route_ref, wind_ref, ice_ref,
-    moved_hbm, gain_ref, damp_ref, force_ref,
-    spec, moved, face_x, face_y, edge_out, edge_in, side_out, side_in,
+    spec_hbm, speed_hbm, ocean_hbm, route_hbm, wind_ref, ice_ref,
+    moved, gain_ref, force_ref,
+    trig_ref, ratio_ref, speed_ref, ocean_ref, route_ref,
+    spec, face_x, face_y, edge_out, edge_in, side_out, side_in,
     ocean_in, ocean_yx, ocean_xy, wind_in, ice_in, table, sums, part, part_in, stage, force_in,
-    load_sem, store_sem, edge_send, edge_recv, side_send, side_recv,
+    load_sem, small_sem, edge_send, edge_recv, side_send, side_recv,
     ocean_send, ocean_recv, wind_send, wind_recv, ice_send, ice_recv,
     part_send, part_recv, force_send, force_recv,
 ):
@@ -42,8 +43,24 @@
     def load(j):
         return pltpu.make_async_copy(spec_hbm.at[j], spec.at[j], load_sem.at[j])
 
+    small = [
+        pltpu.make_async_copy(speed_hbm, speed_ref, small_sem.at[0]),
+        pltpu.make_async_copy(route_hbm, route_ref, small_sem.at[1]),
+        pltpu.make_async_copy(ocean_hbm, ocean_ref, small_sem.at[2]),
+    ]
+    for copy in small:
+        copy.start()
     for j in range(dirs):
         load(j).start()
+    own_lane = pl.multiple_of(((b * capacity) // LANES) * LANES, LANES)
+    own_wind = pltpu.make_async_copy(
+        wind_ref.at[0, :, pl.ds(own_lane, wide)], wind_in.at[b], small_sem.at[3]
+    )
+    own_ice = pltpu.make_async_copy(
+        ice_ref.at[:, pl.ds(own_lane, wide)], ice_in.at[b], small_sem.at[4]
+    )
+    own_wind.start()
+    own_ice.start()
 
     barrier = pltpu.get_barrier_semaphore()
 
@@ -59,6 +76,20 @@
             barrier, inc=1, device_id=(b, lax.rem(d + o, bands)), device_id_type=MESH
         )
 
+    count = dirs * bands
+    for j in range(dirs):
+        for i, wave in enumerate((math.cos, math.sin)):
+            value = jnp.float32(wave(2.0 * math.pi * j / count))
+            for band in range(1, bands):
+                angle = 2.0 * math.pi * (band * dirs + j) / count
+                value = jnp.where(d == band, jnp.float32(wave(angle)), value)
+            trig_ref[i, j] = value
+    for k in range(freqs):
+        for i in range(3):
+            ratio_ref[i, k] = jnp.float32(RATIO_STEP ** ((k - freqs + 1.0) * (i + 2)))
+
+    for copy in small:
+        copy.wait()
     sea = jnp.where(route_ref[...] >= 0, 1.0, 0.0).astype(jnp.float32)
     for side, row in ((0, rows - 1), (1, 0)):
         side_out[side, :freqs, :] = speed_ref[pl.ds(row, freqs, stride=rows), :]
@@ -78,7 +109,7 @@
 
     def ocean_copy(to, src, slot):
         return pltpu.make_async_remote_copy(
-            src_ref=ocean_ref, dst_ref=ocean_in.at[src], send_sem=ocean_send.at[slot],
+            src_ref=ocean_hbm, dst_ref=ocean_in.at[src], send_sem=ocean_send.at[slot],
             recv_sem=ocean_recv.at[src], device_id=(to, d), device_id_type=MESH,
         )
 
@@ -199,14 +230,14 @@
     cur_y = open_y * (flow_y + next_lane(flow_y))
 
     group = 1
-    for size in (6, 5, 4, 3, 2):
+    for size in (12, 9, 6, 4, 3, 2):
         if freqs % size == 0:
             group = size
             break
 
     def one_dir(j, carry):
-        cosine = trig_ref[0, d * dirs + j]
-        sine = trig_ref[1, d * dirs + j]
+        cosine = trig_ref[0, j]
+        sine = trig_ref[1, j]
 
         def some_freqs(g, acc):
             two, three, four = acc
@@ -236,9 +267,8 @@
     lax.fori_loop(0, dirs, one_dir, 0)
 
     high = blocks * tiles
-    own_lane = pl.multiple_of(((b * capacity) // LANES) * LANES, LANES)
-    wind_in[b] = wind_ref[0, :, pl.ds(own_lane, wide)]
-    ice_in[b] = ice_ref[:, pl.ds(own_lane, wide)]
+    own_wind.wait()
+    own_ice.wait()
 
     def wait_winds(o, carry):
         src = lax.rem(b + o, blocks)
@@ -309,8 +339,8 @@
             def _(side=side, c=c):
                 edge_copy(side, c).wait_recv()
         for j in range(c * chunk, (c + 1) * chunk):
-            cosine = trig_ref[0, d * dirs + j]
-            sine = trig_ref[1, d * dirs + j]
+            cosine = trig_ref[0, j]
+            sine = trig_ref[1, j]
             low_speed = low_face * cosine + low_cur
             high_speed = high_face * cosine + high_cur
             low_flux = low_speed * jnp.where(low_speed > 0.0, edge_in[0, j], edge_out[1, j])
@@ -319,7 +349,6 @@
             high_at = pl.ds(rows - 1, freqs, stride=rows)
             moved[j, low_at, :] = moved[j, low_at, :] + low_flux
             moved[j, high_at, :] = moved[j, high_at, :] - high_flux
-            pltpu.make_async_copy(moved.at[j], moved_hbm.at[j], store_sem.at[j]).start()
             fixed = []
             for i in range(3):
                 low_sum = jnp.sum(weights[i] * low_flux, axis=0, keepdims=True)
@@ -370,7 +399,8 @@
         summed = summed + part_in[i]
     steepness = STEEP_COEF * summed[0]
     damping = DAMP_RATE * steepness / (1.0 + steepness)
-    damp_ref[...] = damping
+    for j in range(dirs):
+        gain_ref[j] = gain_ref[j] - damping
     force = summed[1] - damping * summed[2]
 
     square_tile = jnp.concatenate([force, jnp.zeros((LANES - rows, LANES), jnp.float32)], axis=0)
@@ -425,8 +455,6 @@
                 edge_copy(side, c).wait_send()
     for o in range(1, bands):
         part_copy(lax.rem(d + o, bands), d, o).wait_send()
-    for j in range(dirs):
-        pltpu.make_async_copy(moved.at[j], moved_hbm.at[j], store_sem.at[j]).wait()
 
     lax.fori_loop(1, blocks, wait_force, 0)
     for t in range(blocks // per_tile):
@@ -455,29 +483,27 @@
     total = blocks * rows
     padded = (freqs // 8 + 1) * 8
     f32 = jnp.float32
-    count = dirs * bands
-    angles = 2.0 * np.pi * np.arange(count) / count
-    trig = jnp.asarray(np.stack([np.cos(angles), np.sin(angles)]), f32)
     ratios = RATIO_STEP ** (np.arange(freqs) - (freqs - 1.0))
-    ratio_table = jnp.asarray(np.stack([ratios**2, ratios**3, ratios**4]), f32)
     shape = (blocks, bands, dirs, freqs, rows, yrows, chunk)
     vmem = pl.BlockSpec(memory_space=pltpu.VMEM)
-    smem = pl.BlockSpec(memory_space=pltpu.SMEM)
-    anywhere = pl.BlockSpec(memory_space=pl.ANY)
+    hbm = pl.BlockSpec(memory_space=pltpu.HBM)
     dma = pltpu.SemaphoreType.DMA
     force_slots = blocks if yrows % 8 == 0 else 2 * blocks
-    moved, gain, damping, forcing = pl.pallas_call(
+    moved, net, forcing = pl.pallas_call(
         functools.partial(moved_and_sums, shape),
         out_shape=(
-            jax.ShapeDtypeStruct((dirs, freqs * rows, width), f32),
-            jax.ShapeDtypeStruct((dirs, rows, width), f32),
-            jax.ShapeDtypeStruct((rows, width), f32),
-            jax.ShapeDtypeStruct((1, yrows, total), f32),
+            pltpu.VMEM((dirs, freqs * rows, width), f32),
+            pltpu.VMEM((dirs, rows, width), f32),
+            pltpu.VMEM((1, yrows, total), f32),
         ),
-        in_specs=[smem, smem, anywhere, vmem, vmem, vmem, vmem, vmem],
-        out_specs=(anywhere, vmem, vmem, vmem),
+        in_specs=[hbm] * 6,
+        out_specs=(vmem, vmem, vmem),
         scratch_shapes=[
-            pltpu.VMEM((dirs, freqs * rows, width), f32),
+            pltpu.SMEM((2, dirs), f32),
+            pltpu.SMEM((3, freqs), f32),
+            pltpu.VMEM((freqs * rows, width), f32),
+            pltpu.VMEM((2, yrows, total), f32),
+            pltpu.VMEM((rows, width), jnp.int32),
             pltpu.VMEM((dirs, freqs * rows, width), f32),
             pltpu.VMEM((freqs * rows, width), f32),
             pltpu.VMEM((freqs * rows, width), f32),
@@ -496,23 +522,23 @@
             pltpu.VMEM((bands, 3, rows, width), f32),
             pltpu.VMEM((width, LANES), f32),
             pltpu.VMEM((force_slots, yrows, LANES), f32),
-            dma((dirs,)), dma((dirs,)),
+            dma((dirs,)), dma((5,)),
             dma((2, chunks)), dma((2, chunks)), dma((2,)), dma((2,)),
             dma((blocks,)), dma((blocks,)), dma((blocks,)), dma((blocks,)),
             dma((blocks,)), dma((blocks,)),
             dma((bands,)), dma((bands,)), dma((blocks,)), dma((blocks,)),
         ],
         compiler_params=pltpu.CompilerParams(
-            collective_id=0, has_side_effects=True, vmem_limit_bytes=48 * 1024 * 1024
+            collective_id=0, has_side_effects=True, vmem_limit_bytes=60 * 1024 * 1024
         ),
         cost_estimate=pl.CostEstimate(
             flops=30 * spectrum.size, bytes_accessed=8 * spectrum.size, transcendentals=0
         ),
     )(
-        trig, ratio_table, spectrum.reshape(dirs, freqs * rows, width),
+        spectrum.reshape(dirs, freqs * rows, width),
         group_speed.reshape(freqs * rows, width), ocean_current, route_slot, wind_vector, ice_cover,
     )
-    growth = jnp.asarray(ratios, f32)[None, :, None, None] * (gain - damping)[:, None]
+    growth = jnp.asarray(ratios, f32)[None, :, None, None] * net[:, None]
     result = moved.reshape(dirs, freqs, rows, width) * (1.0 + growth)
     return result, forcing
 

time: 42 us -> 29.4 us (0.70)
  local copies, waits for them, and re-layouts: 7.5 us -> 0.6 us
  Pallas kernels: 31.5 us -> 26.1 us
    unnamed x19 -> x3, local copies, waits for them, and re-layouts: 7.5 us -> 0.6 us
    pallas_call x1, Pallas kernels: 31.5 us -> 26.1 us  [on_device(): pl.pallas_call(functools.partial(moved_and_sums, shape), out_shape=(pltpu...]
where the time goes in v2:
time: 29.4 us; the launch traced here: 29.2 us
  Pallas kernels  26.1 us (89%)
  other arithmetic  1.86 us (6%)
  between operations  0.66 us (2%)
  local copies, waits for them, and re-layouts  0.6 us (2%)
    pallas_call x1, Pallas kernels, on_device(): pl.pallas_call(functools.partial(moved_and_sums, shape), out_shape=(pltpu...  26.1 us
    mul x1, other arithmetic, on_device(): result = moved.reshape(dirs, freqs, rows, width) * (1.0 + growth)  1.86 us
    unnamed x3, local copies, waits for them, and re-layouts  0.6 us

profile of v2, /device:TPU:0, one launch (start us, length us, event | category | flops | bytes accessed | tf_op | source)
XLA Modules:
  0.0 29.2 jit_solution(13894271610721841883)
XLA Ops:
  0.6 0.0 copy-start
  0.6 26.1 %shard_map.86 = (f32[9,576,128]{2,1,0:T(8,128)S(1)}, f32[9,16,128]{2,1,0:T(8,128)S(1)}, f32[1,16,128]{2,1,0:T(8,128)S(1)}) custom-call(f32[9,576,128]{2,1,0:T(8,128)} %bitcast.4, f32[576,128]{1,0:T(8,128)} %bitcast.5, f32[2,16,128]{2,1,0:T(8,128)} %ocean_hbm.1, s32[16,128]{1,0:T(8,128)} %route_hbm.1, f32[1,2,2048]{2,1,0:T(2,128)} %wind_ref.1, f32[1,2048]{1,0:T(1,128)} %ice_ref.1), custom_call_target="tpu_custom_call" | custom-call | flops 19906560 | bytes 5308416 | tf_op jit(solution)/shard_map/pallas_call | solution.py:492
  26.8 0.0 copy-done
  26.8 1.9 %add_multiply_fusion = f32[9,36,16,128]{3,2,1,0:T(8,128)} fusion(f32[9,36,16,128]{3,2,1,0:T(8,128)S(1)} %bitcast.3, f32[9,16,128]{2,1,0:T(8,128)S(1)} %get-tuple-element.6, f32[36]{0:T(128)S(1)} %copy-done), kind=kLoop, calls=%fused_computation | loop fusion | flops 1990656 | bytes 5382288 | tf_op jit(solution)/shard_map/mul | solution.py:542
  28.6 0.6 %copy.10 = f32[1,16,128]{2,1,0:T(8,128)} copy(f32[1,16,128]{2,1,0:T(8,128)S(1)} %get-tuple-element.9) | data formatting | bytes 16384
Async XLA Ops:
  0.6 26.1 %copy-start = (f32[36]{0:T(128)S(1)}, f32[36]{0:T(128)}, u32[]{:S(2)}) copy-start(f32[36]{0:T(128)} %constant.4.clone) | copy-start | bytes 436

commit v3 on v2

--- a/solution.py
+++ b/solution.py
@@ -70,7 +70,7 @@
         )
         return carry
 
-    lax.fori_loop(1, blocks, greet_blk, 0)
+    lax.fori_loop(1, blocks, greet_blk, 0, unroll=blocks <= 16)
     for o in range(1, bands):
         pl.semaphore_signal(
             barrier, inc=1, device_id=(b, lax.rem(d + o, bands)), device_id_type=MESH
@@ -139,7 +139,7 @@
         ice_copy(to, b, o).start()
         return carry
 
-    lax.fori_loop(1, blocks, send_ocean, 0)
+    lax.fori_loop(1, blocks, send_ocean, 0, unroll=blocks <= 16)
 
     def side_copy(side):
         return pltpu.make_async_remote_copy(
@@ -172,7 +172,7 @@
             def _(side=side, c=c):
                 edge_copy(side, c).start()
 
-    lax.fori_loop(1, blocks, send_winds, 0)
+    lax.fori_loop(1, blocks, send_winds, 0, unroll=blocks <= 16)
 
     row_id = lax.broadcasted_iota(jnp.int32, (rows, LANES), 0)
     lane_id = lax.broadcasted_iota(jnp.int32, (rows, LANES), 1)
@@ -202,7 +202,7 @@
         ocean_copy(lax.rem(b + o, blocks), lax.rem(b + o, blocks), o).wait_recv()
         return carry
 
-    lax.fori_loop(1, blocks, wait_ocean, 0)
+    lax.fori_loop(1, blocks, wait_ocean, 0, unroll=blocks <= 16)
 
     def lay_ocean(i, carry):
         at = i * yrows
@@ -212,7 +212,7 @@
             ocean_yx[comp, pl.ds(at, yrows), :] = ocean_in[i, comp]
         return carry
 
-    lax.fori_loop(0, blocks, lay_ocean, 0)
+    lax.fori_loop(0, blocks, lay_ocean, 0, unroll=blocks <= 16)
     ocean_xy[:, 0:8, :] = jnp.zeros((2, 8, LANES), jnp.float32)
     total = blocks * rows
     ocean_xy[:, total + 8 : total + 16, :] = jnp.zeros((2, 8, LANES), jnp.float32)
@@ -230,7 +230,7 @@
     cur_y = open_y * (flow_y + next_lane(flow_y))
 
     group = 1
-    for size in (12, 9, 6, 4, 3, 2):
+    for size in (18, 12, 9, 6, 4, 3, 2):
         if freqs % size == 0:
             group = size
             break
@@ -276,7 +276,7 @@
         ice_copy(src, src, o).wait_recv()
         return carry
 
-    lax.fori_loop(1, blocks, wait_winds, 0)
+    lax.fori_loop(1, blocks, wait_winds, 0, unroll=blocks <= 16)
 
     def lay_table(i, carry):
         for t in range(tiles):
@@ -286,7 +286,7 @@
             table[pl.ds(2 * high + i * tiles + t, 1), :] = ice_in[i, :, lanes]
         return carry
 
-    lax.fori_loop(0, blocks, lay_table, 0)
+    lax.fori_loop(0, blocks, lay_table, 0, unroll=blocks <= 16)
     whole = table[...]
     first = whole.astype(jnp.bfloat16)
     rest = whole - first.astype(jnp.float32)
@@ -436,7 +436,7 @@
         force_copy(src, src, o).wait_recv()
         return carry
 
-    lax.fori_loop(1, blocks, send_force, 0)
+    lax.fori_loop(1, blocks, send_force, 0, unroll=blocks <= 16)
     force_in[b] = stage[pl.ds(b * yrows if yrows % 8 else pl.multiple_of(b * yrows, 8), yrows), :]
 
     def drain(o, carry):
@@ -446,7 +446,7 @@
         ice_copy(to, b, o).wait_send()
         return carry
 
-    lax.fori_loop(1, blocks, drain, 0)
+    lax.fori_loop(1, blocks, drain, 0, unroll=blocks <= 16)
     for side, has in sends:
         @pl.when(has)
         def _(side=side):
@@ -456,7 +456,7 @@
     for o in range(1, bands):
         part_copy(lax.rem(d + o, bands), d, o).wait_send()
 
-    lax.fori_loop(1, blocks, wait_force, 0)
+    lax.fori_loop(1, blocks, wait_force, 0, unroll=blocks <= 16)
     for t in range(blocks // per_tile):
         tile = force_in[t * per_tile]
         for i in range(1, per_tile):
@@ -467,7 +467,24 @@
         force_copy(lax.rem(b + o, blocks), b, o).wait_send()
         return carry
 
-    lax.fori_loop(1, blocks, drain_force, 0)
+    lax.fori_loop(1, blocks, drain_force, 0, unroll=blocks <= 16)
+
+
+def finish(ratios, moved, net, force, result_hbm, force_out, buffer, done):
+    dirs, freqs, rows = moved.shape[0], len(ratios), net.shape[1]
+
+    def store(j, slot):
+        return pltpu.make_async_copy(buffer.at[slot], result_hbm.at[j], done.at[slot])
+
+    force_out[...] = force[...]
+    for j in range(dirs):
+        gain = net[j]
+        for k in range(freqs):
+            at = slice(k * rows, (k + 1) * rows)
+            buffer[j, at, :] = moved[j, at, :] * (1.0 + ratios[k] * gain)
+        store(j, j).start()
+    for j in range(dirs):
+        store(j, j).wait()
 
 
 def on_device(spectrum, group_speed, ocean_current, route_slot, wind_vector, ice_cover):
@@ -538,9 +555,18 @@
         spectrum.reshape(dirs, freqs * rows, width),
         group_speed.reshape(freqs * rows, width), ocean_current, route_slot, wind_vector, ice_cover,
     )
-    growth = jnp.asarray(ratios, f32)[None, :, None, None] * net[:, None]
-    result = moved.reshape(dirs, freqs, rows, width) * (1.0 + growth)
-    return result, forcing
+    result, forcing = pl.pallas_call(
+        functools.partial(finish, [float(ratio) for ratio in ratios]),
+        out_shape=(
+            jax.ShapeDtypeStruct((dirs, freqs * rows, width), f32),
+            jax.ShapeDtypeStruct((1, yrows, total), f32),
+        ),
+        in_specs=[vmem, vmem, vmem],
+        out_specs=(hbm, vmem),
+        scratch_shapes=[pltpu.VMEM((dirs, freqs * rows, width), f32), dma((dirs,))],
+        compiler_params=pltpu.CompilerParams(vmem_limit_bytes=16 * 1024 * 1024),
+    )(moved, net, forcing)
+    return result.reshape(dirs, freqs, rows, width), forcing
 
 
 def solution(mesh):

time: 29.4 us -> 28.5 us (0.969)
  other arithmetic: 1.86 us -> 0 us
  Pallas kernels: 26.1 us -> 27.7 us
  local copies, waits for them, and re-layouts: 0.6 us -> 0 us
    pallas_call x0 -> x1, Pallas kernels: none -> 2.2 us  [on_device(): pl.pallas_call(functools.partial(finish, [float(ratio) for ratio in ratio...]
    mul x1 -> x0, other arithmetic: 1.86 us -> none  [on_device(): result = moved.reshape(dirs, freqs, rows, width) * (1.0 + growth)]
    unnamed x3 -> x0, local copies, waits for them, and re-layouts: 0.6 us -> none
    pallas_call x1, Pallas kernels: 26.1 us -> 25.5 us  [on_device(): pl.pallas_call(functools.partial(moved_and_sums, shape), out_shape=(pltpu...]
where the time goes in v3:
time: 28.5 us; the launch traced here: 28.4 us
  Pallas kernels  27.7 us (97%)
  between operations  0.64 us (2%)
    pallas_call x1, Pallas kernels, on_device(): pl.pallas_call(functools.partial(moved_and_sums, shape), out_shape=(pltpu...  25.5 us
    pallas_call x1, Pallas kernels, on_device(): pl.pallas_call(functools.partial(finish, [float(ratio) for ratio in ratio...  2.2 us

profile of v3, /device:TPU:0, one launch (start us, length us, event | category | flops | bytes accessed | tf_op | source)
XLA Modules:
  0.0 28.4 jit_solution(9998577458997166450)
XLA Ops:
  0.6 25.5 %shard_map.77 = (f32[9,576,128]{2,1,0:T(8,128)S(1)}, f32[9,16,128]{2,1,0:T(8,128)S(1)}, f32[1,16,128]{2,1,0:T(8,128)S(1)}) custom-call(f32[9,576,128]{2,1,0:T(8,128)} %bitcast.3, f32[576,128]{1,0:T(8,128)} %bitcast.4, f32[2,16,128]{2,1,0:T(8,128)} %ocean_hbm.1, s32[16,128]{1,0:T(8,128)} %route_hbm.1, f32[1,2,2048]{2,1,0:T(2,128)} %wind_ref.1, f32[1,2048]{1,0:T(1,128)} %ice_ref.1), custom_call_target="tpu_custom_call" | custom-call | flops 19906560 | bytes 5308416 | tf_op jit(solution)/shard_map/pallas_call | solution.py:509
  26.2 2.2 %shard_map.78 = (f32[9,576,128]{2,1,0:T(8,128)}, f32[1,16,128]{2,1,0:T(8,128)}) custom-call(f32[9,576,128]{2,1,0:T(8,128)S(1)} %get-tuple-element.7.moved, f32[9,16,128]{2,1,0:T(8,128)S(1)} %get-tuple-element.8.net, f32[1,16,128]{2,1,0:T(8,128)S(1)} %get-tuple-element.9.force), custom_call_target="tpu_custom_call" | custom-call | tf_op jit(solution)/shard_map/pallas_call | solution.py:558
